TPU v7x, 32 devices: a whole 2x2x4 slice. The times are simulated.
32 devices in a mesh: period: 4 (over z), block: 8 (over y, x, core).
Axes of the slice: x: 2, y: 2, z: 4, core: 2. Of those that a mesh axis runs over, the one named last changes fastest.
Arguments:
- link_rows: bfloat16 [65536, 512], P(('period', 'block')), may hold values from -1.5 to 1.5
- barrier_weights: float32 [65536], P(('period', 'block')), may hold values from 0.1 to 10
- row_residual: float32 [65536], P(('period', 'block')), may hold values from -6 to 6
- tile_pattern: int32 [512, 4], P(('period', 'block')), may hold values 0 or 1
- block_rows: int32 [32], P(('period', 'block')), may hold values from 1 to 2048, 21845 in all
- link_diag: float32 [512], replicated, may hold values from 0.05 to 0.5
Outputs:
- row_step: float32 [65536], P(('period', 'block'))
- link_step: float32 [512], replicated
Inputs may be any that keep to these rules, and one draw needn't show every extreme that they name: `block_rows`: each block has between 1 and 2048 live rows; some block has exactly 2048.
All inputs are finite; a program needn't handle non-finite values. No bound on the sum of `tile_pattern` on one device may be relied on, other than what follows from the above.
Results may differ from a plain program's by a relative error of at most 0.0055.
The roundings to bfloat16 on the way count: a program that leaves them out, or rounds other values in their place, can miss the bound.
Values sent between devices are 32-bit elements; how exact they have to be, the bound alone decides.
A program may use at most 64 MiB of HBM per device.

v0:
```python
import jax
import jax.numpy as jnp
from jax import lax
from jax.sharding import PartitionSpec as P

TILE = 128


def on_device(link_rows, barrier_weights, row_residual, tile_pattern, block_rows, link_diag):
    row_count = link_rows.shape[0]
    width = link_rows.shape[1]
    count = block_rows[0]
    live = (jnp.arange(row_count) < count).astype(jnp.float32)
    cover = jnp.repeat(jnp.repeat(tile_pattern, TILE, axis=0), TILE, axis=1).astype(jnp.float32)
    masked = link_rows * (cover * live[:, None]).astype(jnp.bfloat16)
    scaled = (masked.astype(jnp.float32) * jnp.sqrt(barrier_weights)[:, None]).astype(jnp.bfloat16)
    weighted = (barrier_weights * row_residual * live).astype(jnp.bfloat16)
    tile_count = (count + TILE - 1) // TILE

    def add_tile(index, total):
        first = index * TILE
        piece = lax.dynamic_slice_in_dim(scaled, first, TILE, 0)
        return total + lax.dot_general(
            piece, piece, (((0,), (0,)), ((), ())), preferred_element_type=jnp.float32
        )

    contrib = lax.fori_loop(0, tile_count, add_tile, jnp.zeros((width, width), jnp.float32))
    partial_value = lax.dot_general(
        masked, weighted, (((0,), (0,)), ((), ())), preferred_element_type=jnp.float32
    )
    matrix, vector = (contrib, partial_value)
    owned_rows, owned_vector = (
        lax.psum_scatter(matrix, "block", scatter_dimension=0, tiled=True),
        lax.psum_scatter(vector, "block", scatter_dimension=0, tiled=True),
    )
    owned_rows, owned_vector = lax.psum((owned_rows, owned_vector), "period")
    matrix, vector = (
        lax.all_gather(owned_rows, "block", axis=0, tiled=True),
        lax.all_gather(owned_vector, "block", axis=0, tiled=True),
    )
    schur, gradient = (matrix, vector)
    schur = schur + jnp.diag(link_diag)
    factor = jnp.linalg.cholesky(schur)
    link_step = jax.scipy.linalg.cho_solve((factor, True), gradient)
    step_b = link_step.astype(jnp.bfloat16)
    moved = jnp.dot(masked, step_b, preferred_element_type=jnp.float32)
    row_step = live * barrier_weights * (moved - row_residual)
    return (row_step, link_step)


def solution(mesh):
    return jax.shard_map(
        on_device,
        mesh=mesh,
        in_specs=(
            P(("period", "block"), None),
            P(("period", "block")),
            P(("period", "block")),
            P(("period", "block"), None),
            P(("period", "block")),
            P(),
        ),
        out_specs=(P(("period", "block")), P()),
        check_vma=False,
    )
```

profile of v0, /device:TPU:0, one launch (start us, length us, event | category | flops | bytes accessed | tf_op | source)
XLA Modules:
  0.0 326.3 jit_solution(3742776870668349025)
XLA Ops:
  9.5 4.7 %broadcast_in_dim.32 = f32[2048,4,128]{2,1,0:T(4,128)S(1)} broadcast(f32[2048,4]{1,0:T(8,128)S(1)} %bitcast.160), dimensions={0,1} | broadcast | bytes 4227072 | tf_op jit(solution)/shard_map/broadcast_in_dim | solution.py:14
  14.1 1.9 multiply_convert_fusion
  16.2 5.3 %while.11 = (s32[]{:T(128)}, f32[512,512]{1,0:T(8,128)S(1)}, s32[]{:T(128)}, bf16[2048,512]{1,0:T(8,128)(2,1)}, s32[]{:T(128)}, /*index=5*/s32[]{:T(128)}, s32[]{:T(128)}, s32[]{:T(128)}) while((s32[]{:T(128)}, f32[512,512]{1,0:T(8,128)S(1)}, s32[]{:T(128)}, bf16[2048,512]{1,0:T(8,128)(2,1)}, s32[]{:T(128)}, /*index=5*/s32[]{:T(128)}, ...), condition=%wide.region_1.2_spmd, body=%wide.region_0.1_spmd.sunk | while | flops 67371016 | bytes 2228367 | solution.py:27
  16.2 1.3 convolution_add_fusion.2
  17.5 1.3 convolution_add_fusion.2
  18.9 1.3 convolution_add_fusion.2
  20.2 1.3 convolution_add_fusion.2
  21.5 1.0 copy-done
  22.6 53.4 %reduce-scatter.4.cloned.1.call-done = f32[64,512]{1,0:T(8,128)} async-done(((f32[512,512]{1,0:T(8,128)}), f32[64,512]{1,0:T(8,128)}) %reduce-scatter.4.cloned.1.call-update) | async-done | bytes 131088
  75.9 1.7 copy.37
  77.7 35.8 %all-reduce.5.cloned.1.call-done = f32[64,512]{0,1:T(8,128)} async-done(((f32[64,512]{0,1:T(8,128)}), f32[64,512]{0,1:T(8,128)}) %all-reduce.5.cloned.1.call-update) | async-done | bytes 131088 | tf_op jit(solution)/shard_map/psum | solution.py:36
  113.6 1.7 copy.23
  117.0 12.3 %all-reduce.2 = f32[512]{0:T(512)S(1)} all-reduce(f32[512]{0:T(512)S(1)} %bitcast.164), channel_id=3, replica_groups=mesh['period'=4,'block'=8] {'block'}, use_global_device_ids=true, to_apply=%region_12.13.clone | all-reduce | flops 512 | bytes 4096
  130.0 10.2 %psum.15 = f32[64]{0:T(128)S(1)} all-reduce(f32[64]{0:T(128)S(1)} %dynamic-slice.5), channel_id=1, replica_groups=mesh['period'=4,'block'=8] {'period'}, use_global_device_ids=true, to_apply=%region_13.14 | all-reduce | flops 64 | bytes 512 | tf_op jit(solution)/shard_map/psum | solution.py:36
  140.4 11.9 %all-reduce.1 = f32[512]{0:T(512)S(1)} all-reduce(f32[512]{0:T(512)S(1)} %dynamic-update-slice.23), channel_id=1, replica_groups=mesh['period'=4,'block'=8] {'block'}, use_global_device_ids=true, to_apply=%add.1 | all-reduce | flops 512 | bytes 4096
  152.4 1.6 copy.24
  154.0 1.1 select_add_fusion
  155.1 2.6 copy.25
  157.7 1.4 fusion.16
  159.1 1.0 copy-done.1
  160.1 11.7 %cholesky.103 = f32[128,128]{1,0:T(8,128)S(1)} custom-call(f32[128,128]{1,0:T(8,128)S(1)} %cholesky.263), custom_call_target="Cholesky" | custom-call | tf_op jit(solution)/shard_map/jit(cholesky)/cholesky | solution.py:43
  172.6 9.8 %custom-call.34 = f32[1,128,128]{1,2,0:T(8,128)S(1)} custom-call(f32[1,128,128]{2,1,0:T(8,128)S(1)} %get-tuple-element.75), custom_call_target="InvertDiagBlocksLowerTriangular" | custom-call | tf_op jit(solution)/shard_map/jit(cholesky)/cholesky | solution.py:43
  182.4 1.2 fusion.21
  183.8 1.3 convolution_subtract_fusion
  185.1 11.7 %cholesky.215 = f32[128,128]{1,0:T(8,128)S(1)} custom-call(f32[128,128]{1,0:T(8,128)S(1)} %cholesky.267), custom_call_target="Cholesky" | custom-call | tf_op jit(solution)/shard_map/jit(cholesky)/cholesky | solution.py:43
  196.8 0.7 copy.28
  198.1 1.0 cholesky.222
  199.1 11.4 %custom-call.35 = f32[1,128,128]{1,2,0:T(8,128)} custom-call(f32[1,128,128]{2,1,0:T(8,128)} %get-tuple-element.73), custom_call_target="InvertDiagBlocksLowerTriangular" | custom-call | tf_op jit(solution)/shard_map/jit(cholesky)/cholesky | solution.py:43
  210.5 0.8 constant_dynamic-update-slice_fusion.2
  211.4 1.2 convolution_dynamic-update-slice_fusion
  212.6 1.5 convolution_subtract_fusion.1
  214.1 11.7 %cholesky.236 = f32[128,128]{1,0:T(8,128)S(1)} custom-call(f32[128,128]{1,0:T(8,128)S(1)} %cholesky.272), custom_call_target="Cholesky" | custom-call | tf_op jit(solution)/shard_map/jit(cholesky)/cholesky | solution.py:43
  225.9 9.8 %custom-call.36 = f32[1,128,128]{1,2,0:T(8,128)S(1)} custom-call(f32[1,128,128]{2,1,0:T(8,128)S(1)} %get-tuple-element.71), custom_call_target="InvertDiagBlocksLowerTriangular" | custom-call | tf_op jit(solution)/shard_map/jit(cholesky)/cholesky | solution.py:43
  236.0 1.3 convolution_subtract_fusion.2
  237.4 11.9 %cholesky.253 = f32[128,128]{1,0:T(8,128)S(1)} custom-call(f32[128,128]{1,0:T(8,128)S(1)} %convolution_subtract_fusion.2), custom_call_target="Cholesky" | custom-call | tf_op jit(solution)/shard_map/jit(cholesky)/cholesky | solution.py:43
  254.0 1.1 select_select_fusion
  255.1 14.9 %while.12 = (s32[]{:T(128)}, f32[512,512]{0,1:T(8,128)}, s32[4,2]{0,1:T(2,128)S(1)}, f32[4,128,128]{2,1,0:T(8,128)}, s32[]{:T(128)}) while((s32[]{:T(128)}, f32[512,512]{0,1:T(8,128)}, s32[4,2]{0,1:T(2,128)S(1)}, f32[4,128,128]{2,1,0:T(8,128)}, s32[]{:T(128)}) %tuple.50), condition=%wide.while_cond, body=%wide.while_body.sunk | while | flops 2 | bytes 393329 | solution.py:44
  255.8 2.3 dynamic-slice.12
  259.5 2.3 dynamic-slice.12
  263.2 2.3 dynamic-slice.12
  267.0 2.3 dynamic-slice.12
  270.0 40.1 %custom-call.37 = f32[4,128,128]{1,2,0:T(8,128)S(1)} custom-call(f32[4,128,128]{2,1,0:T(8,128)} %get-tuple-element.33), custom_call_target="InvertDiagBlocksLowerTriangular" | custom-call | tf_op jit(solution)/shard_map/jit(_cho_solve)/triangular_solve | solution.py:44
  310.3 1.0 fusion.9
  311.5 1.1 fusion.10
  312.7 1.2 fusion.15
  314.3 1.1 fusion.6
  315.6 1.1 fusion.11
  316.9 1.2 fusion.13
  (83 shorter events, 15.7 us)
Async XLA Ops:
  7.2 68.8 %reduce-scatter.4.cloned.1.call-start = ((), (), s32[]{:S(2)}) async-start(), calls=%async_computation.3 | async-start | bytes 1179648
  9.4 4.7 %copy-start.2 = (bf16[2048,512]{1,0:T(8,128)(2,1)S(1)}, bf16[2048,512]{1,0:T(8,128)(2,1)}, u32[]{:S(2)}) copy-start(bf16[2048,512]{1,0:T(8,128)(2,1)} %param.8) | copy-start | bytes 6291460
  21.5 1.0 copy-start
  21.5 93.8 %copy-start.7 = (u32[32]{0:T(128)S(1)}, u32[32]{0:T(128)}, u32[]{:S(2)}) copy-start(u32[32]{0:T(128)} %constant.207) | copy-start | bytes 388
  22.5 91.0 %all-reduce.5.cloned.1.call-start = ((), (), s32[]{:S(2)}) async-start(), calls=%async_computation.1 | async-start | bytes 524288 | tf_op jit(solution)/shard_map/psum | solution.py:36
  77.7 74.7 %all-gather.2.cloned.1.call-start = ((), (), s32[]{:S(2)}) async-start(), calls=%async_computation.2 | async-start | bytes 1179648 | tf_op jit(solution)/shard_map/all_gather | solution.py:38
  116.6 37.3 %copy-start.6 = (f32[512]{0:T(512)S(1)}, f32[512]{0:T(512)}, u32[]{:S(2)}) copy-start(f32[512]{0:T(512)} %param.13) | copy-start | bytes 6148
  159.1 1.0 copy-start.1
  270.0 49.1 %copy-start.3 = (f32[2048]{0:T(1024)S(1)}, f32[2048]{0:T(1024)}, u32[]{:S(2)}) copy-start(f32[2048]{0:T(1024)} %param.9) | copy-start | bytes 24580
  270.0 49.1 %copy-start.4 = (f32[2048]{0:T(1024)S(1)}, f32[2048]{0:T(1024)}, u32[]{:S(2)}) copy-start(f32[2048]{0:T(1024)} %param.10) | copy-start | bytes 24580
  318.4 1.3 copy-start.5
Sparse Core Ops, SparseCore 0:
  22.7 53.2 reduce-scatter.3
  78.3 35.2 all-reduce.4
  115.6 23.3 all-gather.1
where the time goes:
time: 328 us; the launch traced here: 326 us
  other arithmetic  129 us (39%)
  waiting for transfers between devices  89.2 us (27%)
  blocking collectives  34.4 us (10%)
  local copies, waits for them, and re-layouts  33.9 us (10%)
  matrix products  21.2 us (6%)
  between operations  18.6 us (6%)
    another operation x14, other arithmetic, on_device(): factor = jnp.linalg.cholesky(schur)  80.8 us
    unnamed x4, waiting for transfers between devices  53.4 us
    another operation x4, other arithmetic, on_device(): link_step = jax.scipy.linalg.cho_solve((factor, True), gradient)  41.3 us
    psum x1, waiting for transfers between devices, on_device(): owned_rows, owned_vector = lax.psum((owned_rows, owned_vector), 'period')  35.8 us
    unnamed x2, blocking collectives  24.2 us
    another operation x20, local copies, waits for them, and re-layouts  14.8 us
    psum x1, blocking collectives, on_device(): owned_rows, owned_vector = lax.psum((owned_rows, owned_vector), 'period')  10.2 us
    another operation x14, matrix products, on_device(): link_step = jax.scipy.linalg.cho_solve((factor, True), gradient)  8.23 us
  transfers between devices with their start and end apart: 3, of which 2 were waited for; matrix products, arithmetic and copies ran while one was open for 0% of the time, Pallas kernels for 0%

commit v1 on v0

v1 whole, which is shorter than its diff:
```python
import functools

import jax
import jax.numpy as jnp
from jax import lax
from jax.experimental import pallas as pl
from jax.experimental.pallas import tpu as pltpu
from jax.sharding import PartitionSpec as P

TILE = 128
SUB = 8
MESH = pl.DeviceIdType.MESH
HIGHEST = lax.Precision.HIGHEST
VMEM = pl.BlockSpec(memory_space=pltpu.VMEM)
SMEM = pl.BlockSpec(memory_space=pltpu.SMEM)
NT = (((1,), (1,)), ((), ()))
TN = (((0,), (0,)), ((), ()))
f32 = jnp.float32
bf16 = jnp.bfloat16


def place(i, j):
    return (i * (i + 1) // 2 + j) * TILE


def live_of(shape, count):
    row = lax.broadcasted_iota(jnp.int32, shape, 0) * TILE + lax.broadcasted_iota(jnp.int32, shape, 1)
    return (row < count).astype(f32)


def cover_of(pattern):
    tiles, blocks = pattern.shape
    return jnp.concatenate(
        [jnp.broadcast_to(pattern[:, c : c + 1], (tiles, TILE)) for c in range(blocks)], axis=1
    ).astype(f32)


def gram_kernel(count_ref, rows_ref, weights_ref, resid_ref, pattern_ref, out_ref, grad_ref, scaled):
    tiles, blocks = pattern_ref.shape
    live = live_of((tiles, TILE), count_ref[0])
    cover = cover_of(pattern_ref[...])
    weights = weights_ref[...]
    weighted = (weights * resid_ref[...] * live).astype(bf16)
    factor = (jnp.sqrt(weights) * live).T
    gradient = jnp.zeros((1, blocks * TILE), f32)
    for t in range(tiles):
        rows = rows_ref[t * TILE : (t + 1) * TILE, :]
        scaled[t * TILE : (t + 1) * TILE, :] = (
            rows.astype(f32) * factor[:, t : t + 1] * cover[t : t + 1, :]
        ).astype(bf16)
        part = jnp.dot(weighted, rows, preferred_element_type=f32)
        gradient = gradient + part[t : t + 1, :] * cover[t : t + 1, :]
    grad_ref[...] = jnp.zeros_like(grad_ref)
    for c in range(blocks):
        grad_ref[c : c + 1, :] = gradient[:, c * TILE : (c + 1) * TILE]
    if out_ref.shape[0] > place(blocks, 0):
        out_ref[place(blocks, 0) :, :] = jnp.zeros((out_ref.shape[0] - place(blocks, 0), TILE), f32)
    for first in range(0, blocks, 2):
        left = scaled[:, first * TILE : (first + 2) * TILE]
        for other in range(0, first + 2, 2):
            right = scaled[:, other * TILE : (other + 2) * TILE]
            piece = lax.dot_general(left, right, TN, preferred_element_type=f32)
            for i in range(2):
                for j in range(2):
                    if first + i >= other + j:
                        at = place(first + i, other + j)
                        out_ref[at : at + TILE, :] = piece[
                            i * TILE : (i + 1) * TILE, j * TILE : (j + 1) * TILE
                        ]


def digits_of(axis, size, whole_up_to):
    if 1 < size <= whole_up_to:
        return [(axis, 1, size)]
    found, stride = [], 1
    while stride < size:
        found.append((axis, stride, 2))
        stride *= 2
    return found


def plan_of(period, block, total):
    near = digits_of("block", block, 1)
    far = digits_of("period", period, 4)
    unit = SUB * period * block
    units = total // unit
    head = (units + 1) // 2
    streams = [(0, head * unit, near + far)]
    if units > head:
        streams.append((head * unit, (units - head) * unit, near[:1] + near[:0:-1] + far))
    return streams


def spread(step):
    axis, stride, size = step
    me = lax.axis_index(axis)
    member = lax.rem(me // stride, size)
    for d in range(1, size):
        to = lax.rem(member + d, size)
        yield d, to, {axis: me + (to - member) * stride}


def sum_kernel(streams, x_ref, g_ref, out_ref, gout_ref, acc, landed, gacc, glanded, send, recv, gsend, grecv):
    barrier = pltpu.get_barrier_semaphore()
    amount = 0
    for step in streams[0][2]:
        for _, _, device in spread(step):
            pl.semaphore_signal(barrier, inc=1, device_id=device, device_id_type=MESH)
            amount += 1
    pl.semaphore_wait(barrier, amount)

    number = [0]
    landing = [0]
    steps = len(streams[0][2])
    begin = [base for base, _, _ in streams]
    extent = [length for _, length, _ in streams]
    held = [[] for _ in streams]
    flight = [None for _ in streams]
    slot = [0]

    def start_scatter(s, k):
        step = streams[s][2][k]
        axis, stride, size = step
        piece = extent[s] // size
        source = x_ref if k == 0 else acc
        copies = []
        for d, to, device in spread(step):
            copy = pltpu.make_async_remote_copy(
                src_ref=source.at[pl.ds(pl.multiple_of(begin[s] + to * piece, SUB), piece)],
                dst_ref=landed.at[pl.ds(landing[0], piece)],
                send_sem=send.at[number[0]],
                recv_sem=recv.at[number[0]],
                device_id=device,
                device_id_type=MESH,
            )
            copy.start()
            copies.append((copy, landing[0]))
            number[0] += 1
            landing[0] += piece
        small = []
        if s == 0:
            for d, to, device in spread(step):
                copy = pltpu.make_async_remote_copy(
                    src_ref=g_ref if k == 0 else gacc.at[k - 1],
                    dst_ref=glanded.at[slot[0]],
                    send_sem=gsend.at[slot[0]],
                    recv_sem=grecv.at[slot[0]],
                    device_id=device,
                    device_id_type=MESH,
                )
                copy.start()
                small.append((copy, slot[0]))
                slot[0] += 1
        flight[s] = (copies, small)

    def end_scatter(s, k):
        axis, stride, size = streams[s][2][k]
        copies, small = flight[s]
        piece = extent[s] // size
        member = lax.rem(lax.axis_index(axis) // stride, size)
        at = pl.multiple_of(begin[s] + member * piece, SUB)
        source = x_ref if k == 0 else acc
        for copy, _ in copies:
            copy.wait()
        total = source[pl.ds(at, piece), :]
        for _, low in copies:
            total = total + landed[pl.ds(low, piece), :]
        (out_ref if k == steps - 1 else acc)[pl.ds(at, piece), :] = total
        held[s].append((begin[s], extent[s]))
        begin[s], extent[s] = at, piece
        if small:
            for copy, _ in small:
                copy.wait()
            total = g_ref[...] if k == 0 else gacc[k - 1]
            for _, low in small:
                total = total + glanded[low]
            if k == steps - 1:
                gout_ref[...] = total
            else:
                gacc[k] = total

    def start_gather(s, k):
        step = streams[s][2][k]
        copies = []
        for d, to, device in spread(step):
            here = out_ref.at[pl.ds(pl.multiple_of(begin[s], SUB), extent[s])]
            copy = pltpu.make_async_remote_copy(
                src_ref=here,
                dst_ref=here,
                send_sem=send.at[number[0]],
                recv_sem=recv.at[number[0]],
                device_id=device,
                device_id_type=MESH,
            )
            copy.start()
            copies.append(copy)
            number[0] += 1
        flight[s] = copies

    def end_gather(s, k):
        for copy in flight[s]:
            copy.wait()
        begin[s], extent[s] = held[s][k]

    every = range(len(streams))
    for s in every:
        start_scatter(s, 0)
    for k in range(steps):
        for s in every:
            end_scatter(s, k)
            if k + 1 < steps:
                start_scatter(s, k + 1)
            else:
                start_gather(s, k)
    for k in reversed(range(steps)):
        for s in every:
            end_gather(s, k)
            if k > 0:
                start_gather(s, k - 1)


def row_of(x, q):
    return jnp.broadcast_to(x[q : q + 1, :], x.shape)


def lane_of(x, j):
    return jnp.broadcast_to(x[:, j : j + 1], x.shape)


def inverse(matrix):
    panels = TILE // SUB
    m = [matrix[i * SUB : (i + 1) * SUB, :] for i in range(panels)]
    lane = lax.broadcasted_iota(jnp.int32, (SUB, TILE), 1)
    sub = lax.broadcasted_iota(jnp.int32, (SUB, TILE), 0)
    for p in range(panels):
        low = p * SUB
        here = (lane >= low) & (lane < low + SUB)
        cols = [lane_of(m[p], low + j) for j in range(SUB)]
        right = jnp.where(here, (lane - low == sub).astype(f32), m[p])
        for q in range(SUB):
            on = sub == q
            pivot = 1.0 / row_of(cols[q], q)
            rest = jnp.where(on, 0.0, cols[q])
            for j in range(q + 1, SUB):
                t = row_of(cols[j], q) * pivot
                cols[j] = jnp.where(on, t, cols[j] - rest * t)
            t = row_of(right, q) * pivot
            right = jnp.where(on, t, right - rest * t)
        fresh = jnp.where(here, -right, right)
        spreads = [row_of(fresh, q) for q in range(SUB)]
        for i in list(range(p + 1, panels)) + list(range(p)):
            terms = [lane_of(m[i], low + q) * spreads[q] for q in range(SUB)]
            while len(terms) > 1:
                terms = [a + b for a, b in zip(terms[::2], terms[1::2])]
            m[i] = jnp.where(here, 0.0, m[i]) - terms[0]
        m[p] = fresh
    return -jnp.concatenate(m, axis=0)


def exact(a, b, dims):
    return lax.dot_general(a, b, dims, precision=HIGHEST, preferred_element_type=f32)


def solve_kernel(
    count_ref, s_ref, g_ref, diag_ref, rows_ref, weights_ref, resid_ref, pattern_ref, step_ref, link_ref, a, w, g
):
    tiles, blocks = pattern_ref.shape
    a[...] = s_ref[: a.shape[0], :]
    g[...] = g_ref[...]
    eye = lax.broadcasted_iota(jnp.int32, (TILE, TILE), 0) == lax.broadcasted_iota(jnp.int32, (TILE, TILE), 1)
    for i in range(blocks):
        at = place(i, i)
        a[at : at + TILE, :] = a[at : at + TILE, :] + jnp.where(eye, diag_ref[i : i + 1, :], 0.0)

    def tile(ref, i, j):
        return ref[place(i, j) : place(i, j) + TILE, :]

    solved = []
    for k in range(blocks):
        inv = inverse(tile(a, k, k))
        own = jnp.broadcast_to(g[k : k + 1, :], (SUB, TILE))
        left = jnp.concatenate([own] + [tile(a, i, k) for i in range(k + 1, blocks)], axis=0)
        moved = exact(left, inv, (((1,), (0,)), ((), ())))
        solved.append(moved[:1, :])
        for i in range(k + 1, blocks):
            at = SUB + (i - k - 1) * TILE
            w[place(i, k) : place(i, k) + TILE, :] = moved[at : at + TILE, :]
        for j in range(k + 1, blocks):
            lower = jnp.concatenate([moved[:SUB, :], moved[SUB + (j - k - 1) * TILE :, :]], axis=0)
            change = exact(lower, tile(a, j, k), NT)
            g[j : j + 1, :] = g[j : j + 1, :] - change[:1, :]
            for i in range(j, blocks):
                at = SUB + (i - j) * TILE
                a[place(i, j) : place(i, j) + TILE, :] = tile(a, i, j) - change[at : at + TILE, :]
    for k in reversed(range(blocks)):
        total = solved[k]
        for i in range(k + 1, blocks):
            x = jnp.broadcast_to(solved[i], (SUB, TILE))
            total = total - exact(x, tile(w, i, k), (((1,), (0,)), ((), ())))[:1, :]
        solved[k] = total
    for k in range(blocks):
        link_ref[k : k + 1, :] = solved[k]

    step = jnp.concatenate(solved, axis=1).astype(bf16).astype(f32)
    steps = (cover_of(pattern_ref[...]) * step).astype(bf16)
    live = live_of((tiles, TILE), count_ref[0])
    scale = live * weights_ref[...]
    resid = resid_ref[...]
    for t in range(tiles):
        moved = lax.dot_general(steps, rows_ref[t * TILE : (t + 1) * TILE, :], NT, preferred_element_type=f32)
        step_ref[t : t + 1, :] = scale[t : t + 1, :] * (moved[t : t + 1, :] - resid[t : t + 1, :])


def on_device(period, block, link_rows, barrier_weights, row_residual, tile_pattern, block_rows, link_diag):
    row_count, width = link_rows.shape
    tiles, blocks = row_count // TILE, width // TILE
    weights = barrier_weights.reshape(tiles, TILE)
    resid = row_residual.reshape(tiles, TILE)
    diag = link_diag.reshape(blocks, TILE)
    unit = SUB * period * block
    used = place(blocks, 0)
    total = -(-used // unit) * unit
    grad_rows = -(-blocks // SUB) * SUB
    limit = pltpu.CompilerParams(vmem_limit_bytes=40 * 1024 * 1024)

    parts, gradient = pl.pallas_call(
        gram_kernel,
        out_shape=(
            jax.ShapeDtypeStruct((total, TILE), f32),
            jax.ShapeDtypeStruct((grad_rows, TILE), f32),
        ),
        in_specs=[SMEM] + [VMEM] * 4,
        out_specs=(VMEM, VMEM),
        scratch_shapes=[pltpu.VMEM((row_count, width), bf16)],
        compiler_params=limit,
        name="gram",
    )(block_rows, link_rows, weights, resid, tile_pattern)

    if period * block > 1:
        streams = plan_of(period, block, total)
        steps = streams[0][2]
        peers = sum(size - 1 for _, _, size in steps)
        landed = 0
        for _, length, order in streams:
            for _, _, size in order:
                length //= size
                landed += length * (size - 1)
        copies = 2 * peers * len(streams)
        parts, gradient = pl.pallas_call(
            functools.partial(sum_kernel, streams),
            out_shape=(
                jax.ShapeDtypeStruct((total, TILE), f32),
                jax.ShapeDtypeStruct((grad_rows, TILE), f32),
            ),
            in_specs=[VMEM, VMEM],
            out_specs=(VMEM, VMEM),
            scratch_shapes=[
                pltpu.VMEM((total, TILE), f32),
                pltpu.VMEM((landed, TILE), f32),
                pltpu.VMEM((len(steps), grad_rows, TILE), f32),
                pltpu.VMEM((peers, grad_rows, TILE), f32),
                pltpu.SemaphoreType.DMA((copies,)),
                pltpu.SemaphoreType.DMA((copies,)),
                pltpu.SemaphoreType.DMA((peers,)),
                pltpu.SemaphoreType.DMA((peers,)),
            ],
            compiler_params=pltpu.CompilerParams(
                collective_id=0, has_side_effects=True, vmem_limit_bytes=40 * 1024 * 1024
            ),
            name="sum_all",
        )(parts, gradient)

    row_step, link_step = pl.pallas_call(
        solve_kernel,
        out_shape=(
            jax.ShapeDtypeStruct((tiles, TILE), f32),
            jax.ShapeDtypeStruct((blocks, TILE), f32),
        ),
        in_specs=[SMEM] + [VMEM] * 7,
        out_specs=(VMEM, VMEM),
        scratch_shapes=[
            pltpu.VMEM((used, TILE), f32),
            pltpu.VMEM((used, TILE), f32),
            pltpu.VMEM((grad_rows, TILE), f32),
        ],
        compiler_params=limit,
        name="solve",
    )(block_rows, parts, gradient, diag, link_rows, weights, resid, tile_pattern)
    return row_step.reshape(row_count), link_step.reshape(width)


def solution(mesh):
    return jax.shard_map(
        functools.partial(on_device, mesh.shape["period"], mesh.shape["block"]),
        mesh=mesh,
        in_specs=(
            P(("period", "block"), None),
            P(("period", "block")),
            P(("period", "block")),
            P(("period", "block"), None),
            P(("period", "block")),
            P(),
        ),
        out_specs=(P(("period", "block")), P()),
        check_vma=False,
    )
```

time: 328 us -> 58.6 us (0.18)
  other arithmetic: 129 us -> 0 us
  waiting for transfers between devices: 89.2 us -> 0 us
  Pallas kernels: 0 us -> 53.2 us
  blocking collectives: 34.4 us -> 0 us
  local copies, waits for them, and re-layouts: 33.9 us -> 3.75 us
  matrix products: 21.2 us -> 0 us
  between operations: 18.6 us -> 1.33 us
    another operation x18 -> x0, other arithmetic: 122 us -> none  [the longest x14 80.8 us: on_device(): factor = jnp.linalg.cholesky(schur)]
    unnamed x4 -> x0, waiting for transfers between devices: 53.4 us -> none
    pallas_call x0 -> x3, Pallas kernels: none -> 53.2 us  [the longest x1 30.5 us: on_device(): pl.pallas_call(functools.partial(sum_kernel, streams), out_shape=(jax.Sha...]
    psum x1 -> x0, waiting for transfers between devices: 35.8 us -> none  [on_device(): owned_rows, owned_vector = lax.psum((owned_rows, owned_vector), 'period')]
    unnamed x2 -> x0, blocking collectives: 24.2 us -> none
    another operation x34 -> x0, local copies, waits for them, and re-layouts: 18.4 us -> none
    another operation x20 -> x0, matrix products: 15 us -> none  [the longest x14 8.23 us: on_device(): link_step = jax.scipy.linalg.cho_solve((factor, True), gradient)]
    psum x1 -> x0, blocking collectives: 10.2 us -> none  [on_device(): owned_rows, owned_vector = lax.psum((owned_rows, owned_vector), 'period')]
  transfers between devices with their start and end apart: 3 -> 0, of which waited for: 2 -> 0; matrix products, arithmetic and copies ran while one was open for 0% -> 0% of each run, Pallas kernels for 0% -> 0%
where the time goes in v1:
time: 58.6 us; the launch traced here: 58.2 us
  Pallas kernels  53.2 us (91%)
  local copies, waits for them, and re-layouts  3.75 us (6%)
  between operations  1.33 us (2%)
    pallas_call x1, Pallas kernels, on_device(): pl.pallas_call(functools.partial(sum_kernel, streams), out_shape=(jax.Sha...  30.5 us
    pallas_call x1, Pallas kernels, on_device(): pl.pallas_call(solve_kernel, out_shape=(jax.ShapeDtypeStruct((tiles, TILE...  21 us
    unnamed x11, local copies, waits for them, and re-layouts  3.75 us
    pallas_call x1, Pallas kernels, on_device(): pl.pallas_call(gram_kernel, out_shape=(jax.ShapeDtypeStruct((total, TILE)...  1.66 us

profile of v1, /device:TPU:0, one launch (start us, length us, event | category | flops | bytes accessed | tf_op | source)
XLA Modules:
  0.0 58.2 jit_solution(10046549100165787917)
XLA Ops:
  0.6 0.0 copy-start.4
  1.3 0.8 %copy.8.pattern_ref = s32[16,4]{1,0:T(8,128)S(1)} copy(s32[16,4]{0,1:T(4,128)} %param.9) | data formatting | bytes 512 | tf_op args[3]
  2.1 0.0 copy-start
  2.1 1.6 %copy-done = bf16[2048,512]{1,0:T(8,128)(2,1)S(1)} copy-done((bf16[2048,512]{1,0:T(8,128)(2,1)S(1)}, bf16[2048,512]{1,0:T(8,128)(2,1)}, u32[]{:S(2)}) %copy-start) | copy-done | bytes 2097176
  3.6 0.0 copy-start.2
  3.7 0.7 %copy-done.2 = f32[2048]{0:T(1024)S(1)} copy-done((f32[2048]{0:T(1024)S(1)}, f32[2048]{0:T(1024)}, u32[]{:S(2)}) %copy-start.2) | copy-done | bytes 8216
  4.3 0.0 copy-start.3
  4.3 0.7 %copy-done.3 = f32[2048]{0:T(1024)S(1)} copy-done((f32[2048]{0:T(1024)S(1)}, f32[2048]{0:T(1024)}, u32[]{:S(2)}) %copy-start.3) | copy-done | bytes 8216
  5.0 0.0 copy-start.1
  5.0 1.7 %gram.1 = (f32[1280,128]{1,0:T(8,128)S(1)}, f32[8,128]{1,0:T(8,128)S(1)}) custom-call(s32[1]{0:T(128)S(6)} %copy.10.count_ref, bf16[2048,512]{1,0:T(8,128)(2,1)S(1)} %copy-done, f32[16,128]{1,0:T(8,128)S(1)} %bitcast.5, f32[16,128]{1,0:T(8,128)S(1)} %bitcast.7, s32[16,4]{1,0:T(8,128)S(1)} %copy.8.pattern_ref), custom_call_target="tpu_custom_call" | custom-call | tf_op jit(solution)/shard_map/gram/pallas_call | solution.py:326
  6.7 30.5 %sum_all.1 = (f32[1280,128]{1,0:T(8,128)S(1)}, f32[8,128]{1,0:T(8,128)S(1)}) custom-call(f32[1280,128]{1,0:T(8,128)S(1)} %get-tuple-element.8.x_ref, f32[8,128]{1,0:T(8,128)S(1)} %get-tuple-element.9.g_ref), custom_call_target="tpu_custom_call" | custom-call | tf_op jit(solution)/shard_map/sum_all/pallas_call | solution.py:349
  37.2 0.0 copy-done.4
  37.2 0.0 copy-done.1
  37.2 21.0 %solve.1 = (f32[16,128]{1,0:T(8,128)}, f32[4,128]{1,0:T(4,128)}) custom-call(s32[1]{0:T(128)S(6)} %copy.10.count_ref, f32[1280,128]{1,0:T(8,128)S(1)} %get-tuple-element.10.s_ref, f32[8,128]{1,0:T(8,128)S(1)} %get-tuple-element.11.g_ref, f32[4,128]{1,0:T(4,128)S(1)} %bitcast.9, bf16[2048,512]{1,0:T(8,128)(2,1)S(1)} %copy-done.1, f32[16,128]{1,0:T(8,128)S(1)} %bitcast.6, ...), custom_call_target="tpu_custom_call" | custom-call | tf_op jit(solution)/shard_map/solve/pallas_call | solution.py:373
Async XLA Ops:
  0.6 36.6 %copy-start.4 = (f32[512]{0:T(512)S(1)}, f32[512]{0:T(512)}, u32[]{:S(2)}) copy-start(f32[512]{0:T(512)} %param.11) | copy-start | bytes 6148
  2.1 1.6 %copy-start = (bf16[2048,512]{1,0:T(8,128)(2,1)S(1)}, bf16[2048,512]{1,0:T(8,128)(2,1)}, u32[]{:S(2)}) copy-start(bf16[2048,512]{1,0:T(8,128)(2,1)} %rows_ref.3) | copy-start | bytes 6291460
  3.6 0.7 %copy-start.2 = (f32[2048]{0:T(1024)S(1)}, f32[2048]{0:T(1024)}, u32[]{:S(2)}) copy-start(f32[2048]{0:T(1024)} %param.7) | copy-start | bytes 24580
  4.3 0.7 %copy-start.3 = (f32[2048]{0:T(1024)S(1)}, f32[2048]{0:T(1024)}, u32[]{:S(2)}) copy-start(f32[2048]{0:T(1024)} %param.8) | copy-start | bytes 24580
  5.0 32.2 %copy-start.1 = (bf16[2048,512]{1,0:T(8,128)(2,1)S(1)}, bf16[2048,512]{1,0:T(8,128)(2,1)}, u32[]{:S(2)}) copy-start(bf16[2048,512]{1,0:T(8,128)(2,1)} %rows_ref.3) | copy-start | bytes 6291460

commit v2 on v0

v2 whole, which is shorter than its diff:
```python
import functools

import jax
import jax.numpy as jnp
from jax import lax
from jax.experimental import pallas as pl
from jax.experimental.pallas import tpu as pltpu
from jax.sharding import PartitionSpec as P

TILE = 128
SUB = 8
MESH = pl.DeviceIdType.MESH
HIGHEST = lax.Precision.HIGHEST
VMEM = pl.BlockSpec(memory_space=pltpu.VMEM)
NT = (((1,), (1,)), ((), ()))
TN = (((0,), (0,)), ((), ()))
f32 = jnp.float32
bf16 = jnp.bfloat16


def layout(blocks):
    order = [(i, j) for j in range(blocks) for i in range(j, blocks)]
    return {pair: n * TILE for n, pair in enumerate(order)}


def live_of(shape, count):
    row = lax.broadcasted_iota(jnp.int32, shape, 0) * TILE + lax.broadcasted_iota(jnp.int32, shape, 1)
    return (row < count).astype(f32)


def cover_of(pattern):
    blocks, tiles = pattern.shape
    eye = lax.broadcasted_iota(jnp.int32, (tiles, tiles), 0) == lax.broadcasted_iota(jnp.int32, (tiles, tiles), 1)
    wide = []
    for c in range(blocks):
        spread_out = jnp.broadcast_to(pattern[c : c + 1, :].astype(f32), (tiles, tiles))
        column = jnp.sum(jnp.where(eye, spread_out, 0.0), axis=1, keepdims=True)
        wide.append(jnp.broadcast_to(column, (tiles, TILE)))
    return jnp.concatenate(wide, axis=1)


def digits_of(axis, size, first):
    found, stride = [], 1
    while stride < size:
        part = min(first if stride == 1 else 4, size // stride)
        found.append((axis, stride, part))
        stride *= part
    return found


def steps_of(period, block):
    return digits_of("block", block, 2) + digits_of("period", period, 4)


def chunks_of(total, unit):
    units = total // unit
    ends = sorted({0, 1, 1 + (units - 1) // 2, units})
    return [(a * unit, (b - a) * unit) for a, b in zip(ends, ends[1:])]


def member_of(step):
    axis, stride, size = step
    return lax.rem(lax.axis_index(axis) // stride, size)


def spread(step):
    axis, stride, size = step
    me = lax.axis_index(axis)
    member = member_of(step)
    for d in range(1, size):
        to = lax.rem(member + d, size)
        yield d, to, {axis: me + (to - member) * stride}


class Sum:
    def __init__(self, steps, base, length, refs, first):
        self.steps, self.refs = steps, refs
        self.begin, self.extent, self.held = base, length, []
        self.number, self.landing = first
        self.flight = []

    def start(self, source, target, device):
        send, recv = self.refs["send"], self.refs["recv"]
        copy = pltpu.make_async_remote_copy(
            src_ref=source,
            dst_ref=target,
            send_sem=send.at[self.number],
            recv_sem=recv.at[self.number],
            device_id=device,
            device_id_type=MESH,
        )
        copy.start()
        self.number += 1
        return copy

    def scatter(self, k):
        piece = self.extent // self.steps[k][2]
        source = self.refs["x" if k == 0 else "acc"]
        self.flight = []
        for _, to, device in spread(self.steps[k]):
            at = pl.multiple_of(self.begin + to * piece, SUB)
            target = self.refs["landed"].at[pl.ds(self.landing, piece)]
            self.flight.append((self.start(source.at[pl.ds(at, piece)], target, device), self.landing))
            self.landing += piece

    def add(self, k):
        piece = self.extent // self.steps[k][2]
        at = pl.multiple_of(self.begin + member_of(self.steps[k]) * piece, SUB)
        total = self.refs["x" if k == 0 else "acc"][pl.ds(at, piece), :]
        for copy, low in self.flight:
            copy.wait()
            total = total + self.refs["landed"][pl.ds(low, piece), :]
        self.refs["out" if k == len(self.steps) - 1 else "acc"][pl.ds(at, piece), :] = total
        self.held.append((self.begin, self.extent))
        self.begin, self.extent = at, piece

    def gather(self, k):
        here = self.refs["out"].at[pl.ds(pl.multiple_of(self.begin, SUB), self.extent)]
        self.flight = [(self.start(here, here, device), 0) for _, _, device in spread(self.steps[k])]

    def land(self, k):
        for copy, _ in self.flight:
            copy.wait()
        self.begin, self.extent = self.held[k]

    def advance(self, turn):
        count = len(self.steps)
        if turn < count:
            self.add(turn)
            if turn + 1 < count:
                self.scatter(turn + 1)
            else:
                self.gather(turn)
        else:
            k = 2 * count - 1 - turn
            self.land(k)
            if k > 0:
                self.gather(k - 1)


class SmallSum:
    def __init__(self, steps, held, send, recv):
        self.steps, self.held, self.send, self.recv = steps, held, send, recv
        self.base, self.number = 0, 0

    def scatter(self, k, value):
        own = self.base + member_of(self.steps[k])
        self.held[own] = value
        self.flight = []
        for _, _, device in spread(self.steps[k]):
            copy = pltpu.make_async_remote_copy(
                src_ref=self.held.at[own],
                dst_ref=self.held.at[own],
                send_sem=self.send.at[self.number],
                recv_sem=self.recv.at[self.number],
                device_id=device,
                device_id_type=MESH,
            )
            copy.start()
            self.flight.append(copy)
            self.number += 1

    def add(self, k):
        for copy in self.flight:
            copy.wait()
        size = self.steps[k][2]
        total = self.held[self.base]
        for n in range(1, size):
            total = total + self.held[self.base + n]
        self.base += size
        return total


def inverse(m, hook):
    lane = lax.broadcasted_iota(jnp.int32, (SUB, TILE), 1)
    sub = lax.broadcasted_iota(jnp.int32, (SUB, TILE), 0)
    wide_lane = lax.broadcasted_iota(jnp.int32, (TILE, TILE), 1)
    for p in range(TILE // SUB):
        hook(p)
        low = p * SUB
        here = (lane >= low) & (lane < low + SUB)
        rows = m[low : low + SUB, :]
        right = jnp.where(here, (lane - low == sub).astype(f32), rows)
        x = jnp.stack(
            [jnp.broadcast_to(rows[:, low + j : low + j + 1], (SUB, TILE)) for j in range(SUB)] + [right], axis=0
        )
        for q in range(SUB):
            on = sub == q
            pivot = 1.0 / jnp.broadcast_to(x[0, q : q + 1, :], (SUB, TILE))
            rest = jnp.where(on, 0.0, x[0])
            later = x[1:]
            t = jnp.broadcast_to(later[:, q : q + 1, :], later.shape) * pivot[None]
            x = jnp.where(on[None], t, later - rest[None] * t)
        fresh = jnp.where(here, -x[0], x[0])
        terms = [
            jnp.broadcast_to(m[:, low + q : low + q + 1], (TILE, TILE))
            * jnp.broadcast_to(fresh[q : q + 1, :], (TILE, TILE))
            for q in range(SUB)
        ]
        while len(terms) > 1:
            terms = [a + b for a, b in zip(terms[::2], terms[1::2])]
        m = jnp.where((wide_lane >= low) & (wide_lane < low + SUB), 0.0, m) - terms[0]
        pieces = [m[:low]] if p else []
        pieces.append(fresh)
        if low + SUB < TILE:
            pieces.append(m[low + SUB :])
        m = jnp.concatenate(pieces, axis=0)
    return -m


def exact(a, b, dims):
    return lax.dot_general(a, b, dims, precision=HIGHEST, preferred_element_type=f32)


NN = (((1,), (0,)), ((), ()))


def whole_kernel(
    steps, chunks, parts,
    count_hbm, rows_hbm, weights_hbm, resid_hbm, pattern_hbm, diag_hbm,
    step_ref, link_ref,
    count_ref, rows_ref, weights_ref, resid_ref, pattern_ref, diag_ref, load,
    scaled, x, acc, landed, out, gheld, send, recv, gsend, grecv, w, g,
):
    blocks, tiles = pattern_ref.shape
    at = layout(blocks)
    used = len(at) * TILE

    if steps:
        barrier = pltpu.get_barrier_semaphore()
        peers = 0
        for step in steps:
            for _, _, device in spread(step):
                pl.semaphore_signal(barrier, inc=1, device_id=device, device_id_type=MESH)
                peers += 1

    few = [
        pltpu.make_async_copy(source, target, load.at[n])
        for n, (source, target) in enumerate(
            [
                (count_hbm, count_ref),
                (weights_hbm, weights_ref),
                (pattern_hbm, pattern_ref),
                (resid_hbm, resid_ref),
                (diag_hbm, diag_ref),
            ]
        )
    ]
    per = tiles // parts
    many = [
        pltpu.make_async_copy(
            rows_hbm.at[pl.ds(n * per * TILE, per * TILE)],
            rows_ref.at[pl.ds(n * per * TILE, per * TILE)],
            load.at[len(few) + n],
        )
        for n in range(parts)
    ]
    for copy in few + many:
        copy.start()
    for copy in few:
        copy.wait()

    live = live_of((tiles, TILE), count_ref[0])
    cover = cover_of(pattern_ref[...])
    weights = weights_ref[...]
    resid = resid_ref[...]
    weighted = (weights * resid * live).astype(bf16)
    factor = (jnp.sqrt(weights) * live).T
    gradient = jnp.zeros((1, blocks * TILE), f32)
    for t in range(tiles):
        if t % per == 0:
            many[t // per].wait()
        rows = rows_ref[t * TILE : (t + 1) * TILE, :]
        scaled[t * TILE : (t + 1) * TILE, :] = (
            rows.astype(f32) * factor[:, t : t + 1] * cover[t : t + 1, :]
        ).astype(bf16)
        part = jnp.dot(weighted, rows, preferred_element_type=f32)
        gradient = gradient + part[t : t + 1, :] * cover[t : t + 1, :]
    g[...] = jnp.zeros_like(g)
    for c in range(blocks):
        g[c : c + 1, :] = gradient[:, c * TILE : (c + 1) * TILE]
    if x.shape[0] > used:
        x[used:, :] = jnp.zeros((x.shape[0] - used, TILE), f32)

    refs = {"x": x, "acc": acc, "landed": landed, "out": out, "send": send, "recv": recv}
    per_chunk = 2 * sum(size - 1 for _, _, size in steps)
    sums, low = [], 0
    for n, (base, length) in enumerate(chunks):
        sums.append(Sum(steps, base, length, refs, (n * per_chunk, low)))
        for _, _, size in steps:
            length //= size
            low += length * (size - 1)

    made, begun = set(), 0
    pairs = [(a, b) for b in range(0, blocks, 2) for a in range(b, blocks, 2)]
    small = None
    for a, b in pairs:
        piece = lax.dot_general(
            scaled[:, a * TILE : (a + 2) * TILE],
            scaled[:, b * TILE : (b + 2) * TILE],
            TN,
            preferred_element_type=f32,
        )
        for i in range(2):
            for j in range(2):
                pair = (a + i, b + j)
                if pair in at:
                    x[at[pair] : at[pair] + TILE, :] = piece[i * TILE : (i + 1) * TILE, j * TILE : (j + 1) * TILE]
                    made.add(pair)
        if not steps:
            continue
        done = min([low for pair, low in at.items() if pair not in made], default=x.shape[0])
        while begun < len(chunks) and sum(chunks[begun]) <= done:
            if begun == 0:
                pl.semaphore_wait(barrier, peers)
                small = SmallSum(steps, gheld, gsend, grecv)
                small.scatter(0, g[...])
            sums[begun].scatter(0)
            begun += 1

    turns = 2 * len(steps)
    queue = []
    if steps:
        for slot in range(turns + 1):
            for n in range(len(sums)):
                turn = slot - (n > 0)
                if 0 <= turn < turns:
                    queue.append((n, turn))
        ready = queue.index((0, turns - 1))
        for n, turn in queue[: ready + 1]:
            if n == 0 and turn < len(steps):
                total = small.add(turn)
                if turn + 1 < len(steps):
                    small.scatter(turn + 1, total)
                else:
                    g[...] = total
            sums[n].advance(turn)
        queue = queue[ready + 1 :]
    matrix = out if steps else x

    def go_on(amount):
        for _ in range(min(amount, len(queue))):
            n, turn = queue.pop(0)
            sums[n].advance(turn)

    eye = lax.broadcasted_iota(jnp.int32, (TILE, TILE), 0) == lax.broadcasted_iota(jnp.int32, (TILE, TILE), 1)

    def tile(ref, i, j):
        return ref[at[i, j] : at[i, j] + TILE, :]

    if sum(chunks[0]) < TILE:
        go_on(len(queue))
    solved = []
    for k in range(blocks):
        hook = (lambda p: go_on(1) if p in (5, 10) else None) if k == 0 else (lambda p: None)
        inv = inverse(tile(matrix, k, k) + jnp.where(eye, diag_ref[k : k + 1, :], 0.0), hook)
        go_on(len(queue))
        own = jnp.broadcast_to(g[k : k + 1, :], (SUB, TILE))
        left = jnp.concatenate([own] + [tile(matrix, i, k) for i in range(k + 1, blocks)], axis=0)
        moved = exact(left, inv, NN)
        solved.append(moved[:1, :])
        for i in range(k + 1, blocks):
            low = SUB + (i - k - 1) * TILE
            w[at[i, k] : at[i, k] + TILE, :] = moved[low : low + TILE, :]
        for j in range(k + 1, blocks):
            lower = jnp.concatenate([moved[:SUB, :], moved[SUB + (j - k - 1) * TILE :, :]], axis=0)
            change = exact(lower, tile(matrix, j, k), NT)
            g[j : j + 1, :] = g[j : j + 1, :] - change[:1, :]
            for i in range(j, blocks):
                low = SUB + (i - j) * TILE
                matrix[at[i, j] : at[i, j] + TILE, :] = tile(matrix, i, j) - change[low : low + TILE, :]
    for k in reversed(range(blocks)):
        total = solved[k]
        for i in range(k + 1, blocks):
            row = jnp.broadcast_to(solved[i], (SUB, TILE))
            total = total - exact(row, tile(w, i, k), NN)[:1, :]
        solved[k] = total
    for k in range(blocks):
        link_ref[k : k + 1, :] = solved[k]

    step = jnp.concatenate(solved, axis=1).astype(bf16).astype(f32)
    masked_steps = (cover * step).astype(bf16)
    scale = live * weights
    for t in range(tiles):
        moved = lax.dot_general(masked_steps, rows_ref[t * TILE : (t + 1) * TILE, :], NT, preferred_element_type=f32)
        step_ref[t : t + 1, :] = scale[t : t + 1, :] * (moved[t : t + 1, :] - resid[t : t + 1, :])


def on_device(period, block, link_rows, barrier_weights, row_residual, tile_pattern, block_rows, link_diag):
    row_count, width = link_rows.shape
    tiles, blocks = row_count // TILE, width // TILE
    unit = SUB * period * block
    total = -(-len(layout(blocks)) * TILE // unit) * unit
    grad_rows = -(-blocks // SUB) * SUB
    steps = steps_of(period, block)
    chunks = chunks_of(total, unit)
    peers = sum(size - 1 for _, _, size in steps)
    slots = sum(size for _, _, size in steps)
    landed = 0
    for _, length in chunks:
        for _, _, size in steps:
            length //= size
            landed += length * (size - 1)
    copies = 2 * peers * len(chunks)
    parts = 4 if tiles % 4 == 0 else 1
    any_space = pl.BlockSpec(memory_space=pltpu.HBM)

    def square(rows):
        return pltpu.VMEM((rows, TILE), f32)

    def semaphores(amount):
        return pltpu.SemaphoreType.DMA((max(amount, 1),))

    row_step, link_step = pl.pallas_call(
        functools.partial(whole_kernel, steps, chunks, parts),
        out_shape=(
            jax.ShapeDtypeStruct((tiles, TILE), f32),
            jax.ShapeDtypeStruct((blocks, TILE), f32),
        ),
        in_specs=[any_space] * 6,
        out_specs=(VMEM, VMEM),
        scratch_shapes=[
            pltpu.SMEM((1,), jnp.int32),
            pltpu.VMEM((row_count, width), bf16),
            square(tiles),
            square(tiles),
            pltpu.VMEM((blocks, tiles), jnp.int32),
            square(blocks),
            semaphores(5 + parts),
            pltpu.VMEM((row_count, width), bf16),
            square(total),
            square(total),
            square(max(landed, SUB)),
            square(total),
            pltpu.VMEM((max(slots, 1), grad_rows, TILE), f32),
            semaphores(copies),
            semaphores(copies),
            semaphores(peers),
            semaphores(peers),
            square(total),
            square(grad_rows),
        ],
        compiler_params=pltpu.CompilerParams(
            collective_id=0, has_side_effects=True, vmem_limit_bytes=60 * 1024 * 1024
        ),
        name="whole",
    )(
        block_rows,
        link_rows,
        barrier_weights.reshape(tiles, TILE),
        row_residual.reshape(tiles, TILE),
        tile_pattern.T,
        link_diag.reshape(blocks, TILE),
    )
    return row_step.reshape(row_count), link_step.reshape(width)


def solution(mesh):
    return jax.shard_map(
        functools.partial(on_device, mesh.shape["period"], mesh.shape["block"]),
        mesh=mesh,
        in_specs=(
            P(("period", "block"), None),
            P(("period", "block")),
            P(("period", "block")),
            P(("period", "block"), None),
            P(("period", "block")),
            P(),
        ),
        out_specs=(P(("period", "block")), P()),
        check_vma=False,
    )
```

time: 328 us -> 49.4 us (0.15)
  other arithmetic: 129 us -> 0 us
  waiting for transfers between devices: 89.2 us -> 0 us
  Pallas kernels: 0 us -> 45.3 us
  blocking collectives: 34.4 us -> 0 us
  local copies, waits for them, and re-layouts: 33.9 us -> 2.53 us
  matrix products: 21.2 us -> 0 us
  between operations: 18.6 us -> 1.29 us
    another operation x18 -> x0, other arithmetic: 122 us -> none  [the longest x14 80.8 us: on_device(): factor = jnp.linalg.cholesky(schur)]
    unnamed x4 -> x0, waiting for transfers between devices: 53.4 us -> none
    pallas_call x0 -> x1, Pallas kernels: none -> 45.3 us  [on_device(): pl.pallas_call(functools.partial(whole_kernel, steps, chunks, parts), out...]
    psum x1 -> x0, waiting for transfers between devices: 35.8 us -> none  [on_device(): owned_rows, owned_vector = lax.psum((owned_rows, owned_vector), 'period')]
    unnamed x2 -> x0, blocking collectives: 24.2 us -> none
    another operation x34 -> x0, local copies, waits for them, and re-layouts: 18.4 us -> none
    another operation x20 -> x0, matrix products: 15 us -> none  [the longest x14 8.23 us: on_device(): link_step = jax.scipy.linalg.cho_solve((factor, True), gradient)]
    psum x1 -> x0, blocking collectives: 10.2 us -> none  [on_device(): owned_rows, owned_vector = lax.psum((owned_rows, owned_vector), 'period')]
  transfers between devices with their start and end apart: 3 -> 0, of which waited for: 2 -> 0; matrix products, arithmetic and copies ran while one was open for 0% -> 0% of each run, Pallas kernels for 0% -> 0%
where the time goes in v2:
time: 49.4 us; the launch traced here: 49.1 us
  Pallas kernels  45.3 us (92%)
  local copies, waits for them, and re-layouts  2.53 us (5%)
  between operations  1.29 us (3%)
    pallas_call x1, Pallas kernels, on_device(): pl.pallas_call(functools.partial(whole_kernel, steps, chunks, parts), out...  45.3 us
    unnamed x2, local copies, waits for them, and re-layouts  2.53 us

profile of v2, /device:TPU:0, one launch (start us, length us, event | category | flops | bytes accessed | tf_op | source)
XLA Modules:
  0.0 49.1 jit_solution(5969301695836943599)
XLA Ops:
  1.3 45.3 %whole.1 = (f32[16,128]{1,0:T(8,128)}, f32[4,128]{1,0:T(4,128)}) custom-call(s32[1]{0:T(128)S(6)} %copy.10.count_hbm, bf16[2048,512]{1,0:T(8,128)(2,1)} %rows_hbm.1, f32[16,128]{1,0:T(8,128)} %bitcast.6, f32[16,128]{1,0:T(8,128)} %bitcast.7, s32[4,16]{1,0:T(4,128)} %bitcast.9, f32[4,128]{1,0:T(4,128)} %bitcast.10), custom_call_target="tpu_custom_call" | custom-call | tf_op jit(solution)/shard_map/whole/pallas_call | solution.py:414
  46.6 1.3 %copy.11 = f32[2048]{0:T(1024)} copy(f32[2048]{0:T(1024)} %bitcast.8) | data formatting | bytes 16384
  47.9 1.2 %copy.12 = f32[512]{0:T(512)} copy(f32[512]{0:T(512)} %bitcast.11) | data formatting | bytes 4096

commit v3 on v2

--- a/solution.py
+++ b/solution.py
@@ -184,13 +184,19 @@
         x = jnp.stack(
             [jnp.broadcast_to(rows[:, low + j : low + j + 1], (SUB, TILE)) for j in range(SUB)] + [right], axis=0
         )
-        for q in range(SUB):
-            on = sub == q
-            pivot = 1.0 / jnp.broadcast_to(x[0, q : q + 1, :], (SUB, TILE))
-            rest = jnp.where(on, 0.0, x[0])
-            later = x[1:]
-            t = jnp.broadcast_to(later[:, q : q + 1, :], later.shape) * pivot[None]
-            x = jnp.where(on[None], t, later - rest[None] * t)
+        for q in range(0, SUB, 2):
+            first, second, later = x[0], x[1], x[2:]
+            a = jnp.broadcast_to(first[q : q + 1, :], (SUB, TILE))
+            b = jnp.broadcast_to(second[q : q + 1, :], (SUB, TILE))
+            d = jnp.broadcast_to(second[q + 1 : q + 2, :], (SUB, TILE))
+            over = 1.0 / (a * d - b * b)
+            u = jnp.broadcast_to(later[:, q : q + 1, :], later.shape)
+            v = jnp.broadcast_to(later[:, q + 1 : q + 2, :], later.shape)
+            tu = d[None] * u - b[None] * v
+            tv = a[None] * v - b[None] * u
+            on_u, on_v = (sub == q)[None], (sub == q + 1)[None]
+            change = jnp.where(on_u, -tu, jnp.where(on_v, -tv, first[None] * tu + second[None] * tv))
+            x = jnp.where(on_u | on_v, 0.0, later) - change * over[None]
         fresh = jnp.where(here, -x[0], x[0])
         terms = [
             jnp.broadcast_to(m[:, low + q : low + q + 1], (TILE, TILE))
@@ -321,9 +327,9 @@
     turns = 2 * len(steps)
     queue = []
     if steps:
-        for slot in range(turns + 1):
+        for slot in range(turns + 3):
             for n in range(len(sums)):
-                turn = slot - (n > 0)
+                turn = slot - (0, 1, 3)[n]
                 if 0 <= turn < turns:
                     queue.append((n, turn))
         ready = queue.index((0, turns - 1))
@@ -345,36 +351,54 @@
 
     eye = lax.broadcasted_iota(jnp.int32, (TILE, TILE), 0) == lax.broadcasted_iota(jnp.int32, (TILE, TILE), 1)
 
+    def need(*wanted):
+        high = max(at[pair] for pair in wanted) + TILE
+        last = min(n for n, chunk in enumerate(chunks) if high <= sum(chunk))
+        while any(n <= last for n, _ in queue):
+            go_on(1)
+
     def tile(ref, i, j):
         return ref[at[i, j] : at[i, j] + TILE, :]
 
-    if sum(chunks[0]) < TILE:
-        go_on(len(queue))
+    def lower(i, j, amount):
+        matrix[at[i, j] : at[i, j] + TILE, :] = tile(matrix, i, j) - amount
+
+    between = {(0, 3): 1, (0, 5): 1, (0, 11): 2, (1, 3): 1, (1, 9): 1}
     solved = []
+
+    def finish_updates(k):
+        for j in range(k + 1, blocks):
+            below = list(range(j + (j == k + 1), blocks))
+            need(*[(i, j) for i in below] + [(j, k)])
+            left = jnp.concatenate([solved[k]] + [tile(w, i, k) for i in below], axis=0)
+            change = exact(left, tile(matrix, j, k), NT)
+            g[j : j + 1, :] = g[j : j + 1, :] - change[:1, :]
+            for n, i in enumerate(below):
+                lower(i, j, change[SUB + n * TILE : SUB + (n + 1) * TILE, :])
+
     for k in range(blocks):
-        hook = (lambda p: go_on(1) if p in (5, 10) else None) if k == 0 else (lambda p: None)
-        inv = inverse(tile(matrix, k, k) + jnp.where(eye, diag_ref[k : k + 1, :], 0.0), hook)
-        go_on(len(queue))
+        need((k, k))
+        diagonal = tile(matrix, k, k) + jnp.where(eye, diag_ref[k : k + 1, :], 0.0)
+        inv = inverse(diagonal, lambda p, k=k: go_on(between.get((k, p), 0)))
+        if k > 0:
+            finish_updates(k - 1)
+        need(*[(i, k) for i in range(k, blocks)])
         own = jnp.broadcast_to(g[k : k + 1, :], (SUB, TILE))
         left = jnp.concatenate([own] + [tile(matrix, i, k) for i in range(k + 1, blocks)], axis=0)
         moved = exact(left, inv, NN)
-        solved.append(moved[:1, :])
+        solved.append(moved[:SUB, :])
         for i in range(k + 1, blocks):
             low = SUB + (i - k - 1) * TILE
             w[at[i, k] : at[i, k] + TILE, :] = moved[low : low + TILE, :]
-        for j in range(k + 1, blocks):
-            lower = jnp.concatenate([moved[:SUB, :], moved[SUB + (j - k - 1) * TILE :, :]], axis=0)
-            change = exact(lower, tile(matrix, j, k), NT)
-            g[j : j + 1, :] = g[j : j + 1, :] - change[:1, :]
-            for i in range(j, blocks):
-                low = SUB + (i - j) * TILE
-                matrix[at[i, j] : at[i, j] + TILE, :] = tile(matrix, i, j) - change[low : low + TILE, :]
+        if k + 1 < blocks:
+            need((k + 1, k + 1))
+            lower(k + 1, k + 1, exact(moved[SUB : SUB + TILE, :], tile(matrix, k + 1, k), NT))
     for k in reversed(range(blocks)):
         total = solved[k]
         for i in range(k + 1, blocks):
-            row = jnp.broadcast_to(solved[i], (SUB, TILE))
-            total = total - exact(row, tile(w, i, k), NN)[:1, :]
+            total = total - exact(solved[i], tile(w, i, k), NN)
         solved[k] = total
+    solved = [row[:1, :] for row in solved]
     for k in range(blocks):
         link_ref[k : k + 1, :] = solved[k]
 
@@ -384,6 +408,17 @@
     for t in range(tiles):
         moved = lax.dot_general(masked_steps, rows_ref[t * TILE : (t + 1) * TILE, :], NT, preferred_element_type=f32)
         step_ref[t : t + 1, :] = scale[t : t + 1, :] * (moved[t : t + 1, :] - resid[t : t + 1, :])
+
+
+def hand_over(row_ref, link_ref, row_out, link_out, sem):
+    copies = [
+        pltpu.make_async_copy(row_ref, row_out, sem.at[0]),
+        pltpu.make_async_copy(link_ref, link_out, sem.at[1]),
+    ]
+    for copy in copies:
+        copy.start()
+    for copy in copies:
+        copy.wait()
 
 
 def on_device(period, block, link_rows, barrier_weights, row_residual, tile_pattern, block_rows, link_diag):
@@ -411,12 +446,13 @@
     def semaphores(amount):
         return pltpu.SemaphoreType.DMA((max(amount, 1),))
 
+    results = (
+        jax.ShapeDtypeStruct((tiles, TILE), f32),
+        jax.ShapeDtypeStruct((blocks, TILE), f32),
+    )
     row_step, link_step = pl.pallas_call(
         functools.partial(whole_kernel, steps, chunks, parts),
-        out_shape=(
-            jax.ShapeDtypeStruct((tiles, TILE), f32),
-            jax.ShapeDtypeStruct((blocks, TILE), f32),
-        ),
+        out_shape=results,
         in_specs=[any_space] * 6,
         out_specs=(VMEM, VMEM),
         scratch_shapes=[
@@ -452,6 +488,15 @@
         tile_pattern.T,
         link_diag.reshape(blocks, TILE),
     )
+    row_step, link_step = pl.pallas_call(
+        hand_over,
+        out_shape=results,
+        in_specs=[any_space, any_space],
+        out_specs=(any_space, any_space),
+        scratch_shapes=[semaphores(2)],
+        compiler_params=pltpu.CompilerParams(vmem_limit_bytes=60 * 1024 * 1024),
+        name="hand_over",
+    )(row_step, link_step)
     return row_step.reshape(row_count), link_step.reshape(width)
 
 

time: 49.4 us -> 53.9 us (1.091)
  Pallas kernels: 45.3 us -> 52.2 us
  local copies, waits for them, and re-layouts: 2.53 us -> 0 us
    pallas_call x1, Pallas kernels: 45.3 us -> 50.8 us  [on_device(): pl.pallas_call(functools.partial(whole_kernel, steps, chunks, parts), out...]
    unnamed x2 -> x0, local copies, waits for them, and re-layouts: 2.53 us -> none
    pallas_call x0 -> x1, Pallas kernels: none -> 1.43 us  [on_device(): pl.pallas_call(hand_over, out_shape=results, in_specs=[any_space, any_spa...]
where the time goes in v3:
time: 53.9 us; the launch traced here: 53.7 us
  Pallas kernels  52.2 us (97%)
  between operations  1.45 us (3%)
    pallas_call x1, Pallas kernels, on_device(): pl.pallas_call(functools.partial(whole_kernel, steps, chunks, parts), out...  50.8 us
    pallas_call x1, Pallas kernels, on_device(): pl.pallas_call(hand_over, out_shape=results, in_specs=[any_space, any_spa...  1.43 us

profile of v3, /device:TPU:0, one launch (start us, length us, event | category | flops | bytes accessed | tf_op | source)
XLA Modules:
  0.0 53.7 jit_solution(14078616850488350088)
XLA Ops:
  1.3 50.8 %whole.1 = (f32[16,128]{1,0:T(8,128)}, f32[4,128]{1,0:T(4,128)}) custom-call(s32[1]{0:T(128)S(6)} %copy.8.count_hbm, bf16[2048,512]{1,0:T(8,128)(2,1)} %rows_hbm.1, f32[16,128]{1,0:T(8,128)} %bitcast.6, f32[16,128]{1,0:T(8,128)} %bitcast.7, s32[4,16]{1,0:T(4,128)} %bitcast.8, f32[4,128]{1,0:T(4,128)} %bitcast.9), custom_call_target="tpu_custom_call" | custom-call | tf_op jit(solution)/shard_map/whole/pallas_call | solution.py:453
  52.1 1.4 %hand_over.1 = (f32[16,128]{1,0:T(8,128)}, f32[4,128]{1,0:T(4,128)}) custom-call(f32[16,128]{1,0:T(8,128)} %get-tuple-element.6.row_ref, f32[4,128]{1,0:T(4,128)} %get-tuple-element.7.link_ref), custom_call_target="tpu_custom_call" | custom-call | tf_op jit(solution)/shard_map/hand_over/pallas_call | solution.py:491

commit v4 on v3

--- a/solution.py
+++ b/solution.py
@@ -58,6 +58,20 @@
     return [(a * unit, (b - a) * unit) for a, b in zip(ends, ends[1:])]
 
 
+def swaps_last(steps, chunks):
+    return len(chunks) > 1 and len(steps) > 1
+
+
+def landing_rows(steps, length, swap):
+    amount = 0
+    for k, (_, _, size) in enumerate(steps):
+        if swap and k == len(steps) - 1:
+            return amount + length * size
+        length //= size
+        amount += length * (size - 1)
+    return amount
+
+
 def member_of(step):
     axis, stride, size = step
     return lax.rem(lax.axis_index(axis) // stride, size)
@@ -73,8 +87,9 @@
 
 
 class Sum:
-    def __init__(self, steps, base, length, refs, first):
-        self.steps, self.refs = steps, refs
+    def __init__(self, steps, base, length, refs, first, swap):
+        self.steps, self.refs, self.swap = steps, refs, swap
+        self.turns = 2 * len(steps) - swap
         self.begin, self.extent, self.held = base, length, []
         self.number, self.landing = first
         self.flight = []
@@ -118,21 +133,41 @@
         here = self.refs["out"].at[pl.ds(pl.multiple_of(self.begin, SUB), self.extent)]
         self.flight = [(self.start(here, here, device), 0) for _, _, device in spread(self.steps[k])]
 
+    def exchange(self, k):
+        size = self.steps[k][2]
+        own = pl.ds(pl.multiple_of(self.landing + member_of(self.steps[k]) * self.extent, SUB), self.extent)
+        here = self.refs["landed"].at[own]
+        self.refs["landed"][own, :] = self.refs["acc"][pl.ds(pl.multiple_of(self.begin, SUB), self.extent), :]
+        self.flight = [(self.start(here, here, device), 0) for _, _, device in spread(self.steps[k])]
+
+    def add_exchanged(self, k):
+        for copy, _ in self.flight:
+            copy.wait()
+        total = self.refs["landed"][pl.ds(self.landing, self.extent), :]
+        for n in range(1, self.steps[k][2]):
+            total = total + self.refs["landed"][pl.ds(self.landing + n * self.extent, self.extent), :]
+        self.refs["out"][pl.ds(pl.multiple_of(self.begin, SUB), self.extent), :] = total
+
     def land(self, k):
         for copy, _ in self.flight:
             copy.wait()
         self.begin, self.extent = self.held[k]
 
     def advance(self, turn):
-        count = len(self.steps)
-        if turn < count:
+        last = len(self.steps) - 1
+        if self.swap and turn == last:
+            self.add_exchanged(last)
+            self.gather(last - 1)
+        elif turn <= last:
             self.add(turn)
-            if turn + 1 < count:
+            if turn == last:
+                self.gather(last)
+            elif self.swap and turn + 1 == last:
+                self.exchange(last)
+            else:
                 self.scatter(turn + 1)
-            else:
-                self.gather(turn)
         else:
-            k = 2 * count - 1 - turn
+            k = self.turns - 1 - turn
             self.land(k)
             if k > 0:
                 self.gather(k - 1)
@@ -292,10 +327,9 @@
     per_chunk = 2 * sum(size - 1 for _, _, size in steps)
     sums, low = [], 0
     for n, (base, length) in enumerate(chunks):
-        sums.append(Sum(steps, base, length, refs, (n * per_chunk, low)))
-        for _, _, size in steps:
-            length //= size
-            low += length * (size - 1)
+        swap = int(swaps_last(steps, chunks) and n == 0)
+        sums.append(Sum(steps, base, length, refs, (n * per_chunk, low), swap))
+        low += landing_rows(steps, length, swap)
 
     made, begun = set(), 0
     pairs = [(a, b) for b in range(0, blocks, 2) for a in range(b, blocks, 2)]
@@ -324,15 +358,14 @@
             sums[begun].scatter(0)
             begun += 1
 
-    turns = 2 * len(steps)
     queue = []
     if steps:
-        for slot in range(turns + 3):
-            for n in range(len(sums)):
-                turn = slot - (0, 1, 3)[n]
-                if 0 <= turn < turns:
-                    queue.append((n, turn))
-        ready = queue.index((0, turns - 1))
+        final = sums[0].turns - 1
+        queue = sorted(
+            ((n, turn) for n, one in enumerate(sums) for turn in range(one.turns)),
+            key=lambda item: (item[1] - (item == (0, final)), item[0], item[1]),
+        )
+        ready = queue.index((0, final))
         for n, turn in queue[: ready + 1]:
             if n == 0 and turn < len(steps):
                 total = small.add(turn)
@@ -363,7 +396,7 @@
     def lower(i, j, amount):
         matrix[at[i, j] : at[i, j] + TILE, :] = tile(matrix, i, j) - amount
 
-    between = {(0, 3): 1, (0, 5): 1, (0, 11): 2, (1, 3): 1, (1, 9): 1}
+    between = {(0, 4): 1, (0, 6): 1, (0, 13): 1, (0, 15): 1, (1, 3): 1}
     solved = []
 
     def finish_updates(k):
@@ -432,10 +465,8 @@
     peers = sum(size - 1 for _, _, size in steps)
     slots = sum(size for _, _, size in steps)
     landed = 0
-    for _, length in chunks:
-        for _, _, size in steps:
-            length //= size
-            landed += length * (size - 1)
+    for n, (_, length) in enumerate(chunks):
+        landed += landing_rows(steps, length, swaps_last(steps, chunks) and n == 0)
     copies = 2 * peers * len(chunks)
     parts = 4 if tiles % 4 == 0 else 1
     any_space = pl.BlockSpec(memory_space=pltpu.HBM)

time: 53.9 us -> 45.3 us (0.84)
  Pallas kernels: 52.2 us -> 43.7 us
    pallas_call x1, Pallas kernels: 50.8 us -> 42.2 us  [on_device(): pl.pallas_call(functools.partial(whole_kernel, steps, chunks, parts), out...]
where the time goes in v4:
time: 45.3 us; the launch traced here: 45.1 us
  Pallas kernels  43.7 us (96%)
  between operations  1.45 us (3%)
    pallas_call x1, Pallas kernels, on_device(): pl.pallas_call(functools.partial(whole_kernel, steps, chunks, parts), out...  42.2 us
    pallas_call x1, Pallas kernels, on_device(): pl.pallas_call(hand_over, out_shape=results, in_specs=[any_space, any_spa...  1.43 us

profile of v4, /device:TPU:0, one launch (start us, length us, event | category | flops | bytes accessed | tf_op | source)
XLA Modules:
  0.0 45.1 jit_solution(7915969674967423721)
XLA Ops:
  1.3 42.2 %whole.1 = (f32[16,128]{1,0:T(8,128)}, f32[4,128]{1,0:T(4,128)}) custom-call(s32[1]{0:T(128)S(6)} %copy.8.count_hbm, bf16[2048,512]{1,0:T(8,128)(2,1)} %rows_hbm.1, f32[16,128]{1,0:T(8,128)} %bitcast.6, f32[16,128]{1,0:T(8,128)} %bitcast.7, s32[4,16]{1,0:T(4,128)} %bitcast.8, f32[4,128]{1,0:T(4,128)} %bitcast.9), custom_call_target="tpu_custom_call" | custom-call | tf_op jit(solution)/shard_map/whole/pallas_call | solution.py:484
  43.5 1.4 %hand_over.1 = (f32[16,128]{1,0:T(8,128)}, f32[4,128]{1,0:T(4,128)}) custom-call(f32[16,128]{1,0:T(8,128)} %get-tuple-element.6.row_ref, f32[4,128]{1,0:T(4,128)} %get-tuple-element.7.link_ref), custom_call_target="tpu_custom_call" | custom-call | tf_op jit(solution)/shard_map/hand_over/pallas_call | solution.py:522

commit v5 on v4

--- a/solution.py
+++ b/solution.py
@@ -363,17 +363,17 @@
         final = sums[0].turns - 1
         queue = sorted(
             ((n, turn) for n, one in enumerate(sums) for turn in range(one.turns)),
-            key=lambda item: (item[1] - (item == (0, final)), item[0], item[1]),
+            key=lambda item: (final - 1, 1.5) if item == (0, final) else (item[1] + item[0] // 2, item[0]),
         )
         ready = queue.index((0, final))
         for n, turn in queue[: ready + 1]:
+            sums[n].advance(turn)
             if n == 0 and turn < len(steps):
                 total = small.add(turn)
                 if turn + 1 < len(steps):
                     small.scatter(turn + 1, total)
                 else:
                     g[...] = total
-            sums[n].advance(turn)
         queue = queue[ready + 1 :]
     matrix = out if steps else x
 
@@ -396,7 +396,7 @@
     def lower(i, j, amount):
         matrix[at[i, j] : at[i, j] + TILE, :] = tile(matrix, i, j) - amount
 
-    between = {(0, 4): 1, (0, 6): 1, (0, 13): 1, (0, 15): 1, (1, 3): 1}
+    between = {(0, 2): 1, (0, 6): 1, (0, 10): 1, (1, 2): 1, (1, 9): 1}
     solved = []
 
     def finish_updates(k):

time: 45.3 us -> 47.5 us (1.049)
  Pallas kernels: 43.7 us -> 45.8 us
    pallas_call x1, Pallas kernels: 42.2 us -> 44.4 us  [on_device(): pl.pallas_call(functools.partial(whole_kernel, steps, chunks, parts), out...]
where the time goes in v5:
time: 47.5 us; the launch traced here: 47.3 us
  Pallas kernels  45.8 us (96%)
  between operations  1.45 us (3%)
    pallas_call x1, Pallas kernels, on_device(): pl.pallas_call(functools.partial(whole_kernel, steps, chunks, parts), out...  44.4 us
    pallas_call x1, Pallas kernels, on_device(): pl.pallas_call(hand_over, out_shape=results, in_specs=[any_space, any_spa...  1.43 us

profile of v5, /device:TPU:0, one launch (start us, length us, event | category | flops | bytes accessed | tf_op | source)
XLA Modules:
  0.0 47.3 jit_solution(11898517200281578063)
XLA Ops:
  1.3 44.4 %whole.1 = (f32[16,128]{1,0:T(8,128)}, f32[4,128]{1,0:T(4,128)}) custom-call(s32[1]{0:T(128)S(6)} %copy.8.count_hbm, bf16[2048,512]{1,0:T(8,128)(2,1)} %rows_hbm.1, f32[16,128]{1,0:T(8,128)} %bitcast.6, f32[16,128]{1,0:T(8,128)} %bitcast.7, s32[4,16]{1,0:T(4,128)} %bitcast.8, f32[4,128]{1,0:T(4,128)} %bitcast.9), custom_call_target="tpu_custom_call" | custom-call | tf_op jit(solution)/shard_map/whole/pallas_call | solution.py:484
  45.7 1.4 %hand_over.1 = (f32[16,128]{1,0:T(8,128)}, f32[4,128]{1,0:T(4,128)}) custom-call(f32[16,128]{1,0:T(8,128)} %get-tuple-element.6.row_ref, f32[4,128]{1,0:T(4,128)} %get-tuple-element.7.link_ref), custom_call_target="tpu_custom_call" | custom-call | tf_op jit(solution)/shard_map/hand_over/pallas_call | solution.py:522

commit v6 on v4

--- a/solution.py
+++ b/solution.py
@@ -396,7 +396,7 @@
     def lower(i, j, amount):
         matrix[at[i, j] : at[i, j] + TILE, :] = tile(matrix, i, j) - amount
 
-    between = {(0, 4): 1, (0, 6): 1, (0, 13): 1, (0, 15): 1, (1, 3): 1}
+    between = {(0, 1): 1, (0, 3): 1, (0, 9): 1, (0, 12): 1, (1, 2): 1}
     solved = []
 
     def finish_updates(k):

time: 45.3 us -> 45.4 us (level)
  no operation moved by 1% of the time
where the time goes in v6:
time: 45.4 us; the launch traced here: 45.2 us
  Pallas kernels  43.8 us (96%)
  between operations  1.45 us (3%)
    pallas_call x1, Pallas kernels, on_device(): pl.pallas_call(functools.partial(whole_kernel, steps, chunks, parts), out...  42.3 us
    pallas_call x1, Pallas kernels, on_device(): pl.pallas_call(hand_over, out_shape=results, in_specs=[any_space, any_spa...  1.43 us

profile of v6, /device:TPU:0, one launch (start us, length us, event | category | flops | bytes accessed | tf_op | source)
XLA Modules:
  0.0 45.2 jit_solution(14394655338067730007)
XLA Ops:
  1.3 42.3 %whole.1 = (f32[16,128]{1,0:T(8,128)}, f32[4,128]{1,0:T(4,128)}) custom-call(s32[1]{0:T(128)S(6)} %copy.8.count_hbm, bf16[2048,512]{1,0:T(8,128)(2,1)} %rows_hbm.1, f32[16,128]{1,0:T(8,128)} %bitcast.6, f32[16,128]{1,0:T(8,128)} %bitcast.7, s32[4,16]{1,0:T(4,128)} %bitcast.8, f32[4,128]{1,0:T(4,128)} %bitcast.9), custom_call_target="tpu_custom_call" | custom-call | tf_op jit(solution)/shard_map/whole/pallas_call | solution.py:484
  43.6 1.4 %hand_over.1 = (f32[16,128]{1,0:T(8,128)}, f32[4,128]{1,0:T(4,128)}) custom-call(f32[16,128]{1,0:T(8,128)} %get-tuple-element.6.row_ref, f32[4,128]{1,0:T(4,128)} %get-tuple-element.7.link_ref), custom_call_target="tpu_custom_call" | custom-call | tf_op jit(solution)/shard_map/hand_over/pallas_call | solution.py:522
